TPU v7x, 256 devices: a whole 4x4x8 slice. The times are simulated.
256 devices in a mesh: ctx: 32 (over z, x), tp: 8 (over y, core).
Axes of the slice: x: 4, y: 4, z: 8, core: 2. Of those that a mesh axis runs over, the one named last changes fastest.
Arguments:
- queries: bfloat16 [16384, 4096], P('ctx', 'tp'), may hold values from -90 to 90
- key_states: bfloat16 [16384, 1024], P('ctx', 'tp'), may hold values from -3 to 3
- values: bfloat16 [16384, 1024], P('ctx', 'tp'), may hold values from -6 to 6
- out_grad: bfloat16 [16384, 4096], P('ctx', 'tp'), may hold values from -6 to 6
- weight: bfloat16 [4096, 6144], P(None, 'tp'), may hold values from -0.09375 to 0.09375
- lengths: int32 [64], replicated, may hold values from 128 to 384, as said below
- block_plan: int32 [128], replicated, may hold values from 0 to 31, as said below
Outputs:
- attention_out: bfloat16 [16384, 4096], P('ctx', 'tp')
- grad_input: bfloat16 [16384, 4096], P('ctx', 'tp')
- log_sum_exp: float32 [32, 16384], P('tp', 'ctx')
Inputs may be any that keep to these rules, and one draw needn't show every extreme that they name: `lengths`: the documents lie end to end in window order and together hold 16384 tokens; every length is a whole number of blocks of 128 tokens, so documents begin and end at block bounds. `block_plan`: entry b is the device of ctx that block b of the window (tokens b * 128 to b * 128 + 127) goes to. All blocks of one document go to one device, and every device receives exactly 4 blocks. A block goes to the device that holds it in the window or to the next or previous index of ctx (no wrap). A device sends at most 3 blocks to each of its two neighbours, and in every draw some device sends 3 blocks to the next index.
All inputs are finite; a program needn't handle non-finite values.
Results may differ from a plain program's by a relative error of at most 0.033.
Values may be sent and summed in bfloat16 or wider, within the bound.
A program may use at most 64 MiB of HBM per device.

v0:
```python
import jax
import jax.numpy as jnp
from jax import lax
from jax.sharding import PartitionSpec as P

HEAD_DIM = 128
BLOCK = 128
GROUP = 4


def padded(cells, sides, width):
    for axis, dim in sides:
        count = lax.axis_size(axis)
        ends = count - 1
        head = lax.slice_in_dim(cells, 0, width, axis=dim)
        tail = lax.slice_in_dim(cells, cells.shape[dim] - width, cells.shape[dim], axis=dim)
        cells = jnp.concatenate(
            [
                lax.ppermute(tail, axis, [(i, (i + 1) % count) for i in range(ends)]),
                cells,
                lax.ppermute(head, axis, [((i + 1) % count, i) for i in range(ends)]),
            ],
            axis=dim,
        )
    return cells


def doc_index(lengths, positions):
    bounds = jnp.cumsum(lengths)
    return jnp.sum((positions[:, None] >= bounds[None, :]).astype(jnp.int32), axis=1)


def select_rows(table, rows):
    return jnp.dot(
        table.astype(rows.dtype),
        rows,
        preferred_element_type=jnp.float32,
        precision=lax.Precision.HIGHEST,
    )


def attend(queries, key_rows, value_rows, out_grad, query_pos, query_doc, key_pos, key_doc):
    rows_total = queries.shape[0]
    groups = key_rows.shape[1] // HEAD_DIM
    block_rows = min(512, rows_total)
    block_total = rows_total // block_rows
    scale = HEAD_DIM ** (-0.5)
    key_heads = key_rows.reshape(-1, groups, HEAD_DIM)
    value_heads = value_rows.reshape(-1, groups, HEAD_DIM)
    query_blocks = queries.reshape(block_total, block_rows, groups, GROUP, HEAD_DIM)
    grad_blocks = out_grad.reshape(block_total, block_rows, groups, GROUP, HEAD_DIM)
    pos_blocks = query_pos.reshape(block_total, block_rows)
    doc_blocks = query_doc.reshape(block_total, block_rows)
    starts = jnp.arange(block_total, dtype=jnp.int32) * block_rows

    def one_block(carry, item):
        key_sum, value_sum = carry
        query_part, grad_part, pos_part, doc_part, start = item
        scores = (
            jnp.einsum("qgjd,kgd->gjqk", query_part, key_heads, preferred_element_type=jnp.float32)
            * scale
        )
        allowed = (
            (doc_part[:, None] == key_doc[None, :])
            & (key_pos[None, :] <= pos_part[:, None])
            & (key_pos[None, :] >= 0)
        )
        scores = jnp.where(allowed, scores, -jnp.inf)
        top = jnp.max(scores, axis=-1, keepdims=True)
        raised = jnp.exp(scores - top)
        row_sum = jnp.sum(raised, axis=-1, keepdims=True)
        weights = raised / row_sum
        row_lse = (top + jnp.log(row_sum))[..., 0]
        weights_low = weights.astype(jnp.bfloat16)
        result = jnp.einsum(
            "gjqk,kgd->qgjd", weights_low, value_heads, preferred_element_type=jnp.float32
        ).astype(jnp.bfloat16)
        row_dot = jnp.sum(grad_part.astype(jnp.float32) * result.astype(jnp.float32), axis=-1)
        prob_grad = jnp.einsum(
            "qgjd,kgd->gjqk", grad_part, value_heads, preferred_element_type=jnp.float32
        )
        score_grad = (
            weights * (prob_grad - jnp.transpose(row_dot, (1, 2, 0))[..., None]) * scale
        ).astype(jnp.bfloat16)
        query_grad = jnp.einsum(
            "gjqk,kgd->qgjd", score_grad, key_heads, preferred_element_type=jnp.float32
        ).astype(jnp.bfloat16)
        key_add = jnp.einsum(
            "gjqk,qgjd->kgd", score_grad, query_part, preferred_element_type=jnp.float32
        )
        value_add = jnp.einsum(
            "gjqk,qgjd->kgd", weights_low, grad_part, preferred_element_type=jnp.float32
        )
        key_sum = key_sum + key_add
        value_sum = value_sum + value_add
        return ((key_sum, value_sum), (result, row_lse, query_grad))

    empty = jnp.zeros((key_heads.shape[0], groups, HEAD_DIM), jnp.float32)
    sums, outputs = lax.scan(
        one_block, (empty, empty), (query_blocks, grad_blocks, pos_blocks, doc_blocks, starts)
    )
    result = outputs[0].reshape(rows_total, groups * GROUP * HEAD_DIM)
    row_lse = jnp.transpose(outputs[1], (1, 2, 0, 3)).reshape(groups * GROUP, rows_total)
    query_grad = outputs[2].reshape(rows_total, groups * GROUP * HEAD_DIM)
    return (
        result,
        row_lse,
        query_grad,
        sums[0].reshape(key_heads.shape[0], -1),
        sums[1].reshape(key_heads.shape[0], -1),
    )


def project(query_grad, key_grad, value_grad, weight):
    pieces = []
    pieces.append(query_grad)
    pieces.append(key_grad)
    pieces.append(value_grad)
    stacked = jnp.concatenate(pieces, axis=1)
    summed = lax.psum_scatter(
        lax.dot_general(
            weight, stacked, (((1,), (1,)), ((), ())), preferred_element_type=jnp.float32
        ).astype(jnp.bfloat16),
        "tp",
        scatter_dimension=0,
        tiled=True,
    ).astype(jnp.float32)
    return jnp.transpose(summed).astype(jnp.bfloat16)


def body(queries, key_states, values, out_grad, weight, lengths, block_plan):
    tok_rows = queries.shape[0]
    key_width = key_states.shape[1]
    query_width = queries.shape[1]
    blocks = tok_rows // BLOCK
    reach = (blocks - 2) * BLOCK
    spare = blocks - 1
    my_index = lax.axis_index("ctx")
    total_blocks = block_plan.shape[0]
    block_ids = jnp.arange(total_blocks, dtype=jnp.int32)
    slots = jnp.arange(blocks, dtype=jnp.int32)
    places = jnp.arange(spare, dtype=jnp.int32)
    own_plan = lax.dynamic_slice_in_dim(block_plan, my_index * blocks, blocks)

    def outgoing(target):
        hits = (own_plan == target).astype(jnp.int32)
        order = jnp.cumsum(hits) - hits
        return (hits[None, :] == 1) & (order[None, :] == places[:, None])

    to_prev = outgoing(my_index - 1)
    to_next = outgoing(my_index + 1)
    mine = (block_plan == my_index).astype(jnp.int32)
    rank = jnp.cumsum(mine) - mine
    picked = (mine[None, :] == 1) & (rank[None, :] == slots[:, None])
    source = jnp.sum(jnp.where(picked, block_ids[None, :], 0), axis=1)
    source_dev = source // blocks
    source_slot = source % blocks
    earlier = (source_dev[:, None] == source_dev[None, :]) & (slots[None, :] < slots[:, None])
    turn = jnp.sum(earlier.astype(jnp.int32), axis=1)
    from_prev = (source_dev[:, None] == my_index - 1) & (turn[:, None] == places[None, :])
    from_next = (source_dev[:, None] == my_index + 1) & (turn[:, None] == places[None, :])
    keep_table = (source_dev[:, None] == my_index) & (source_slot[:, None] == slots[None, :])
    packed = jnp.concatenate([queries, key_states, values, out_grad], axis=1).reshape(blocks, -1)
    leaving = jnp.concatenate(
        [select_rows(to_prev, packed), select_rows(to_next, packed)], 0
    ).astype(jnp.bfloat16)
    arrived = padded(leaving, (("ctx", 0),), spare)
    moved = (
        select_rows(from_prev, arrived[:spare])
        + select_rows(keep_table, packed)
        + select_rows(from_next, arrived[3 * spare :])
    )
    moved = moved.astype(jnp.bfloat16).reshape(tok_rows, -1)
    moved_query = moved[:, :query_width]
    moved_key = moved[:, query_width : query_width + key_width]
    moved_value = moved[:, query_width + key_width : query_width + 2 * key_width]
    moved_grad = moved[:, query_width + 2 * key_width :]
    relaid_pos = (source[:, None] * BLOCK + jnp.arange(BLOCK, dtype=jnp.int32)[None, :]).reshape(-1)
    relaid_doc = doc_index(lengths, relaid_pos)
    filler = jnp.zeros((reach, key_width), jnp.bfloat16)
    wide_key = jnp.concatenate([filler, moved_key], 0)
    wide_value = jnp.concatenate([filler, moved_value], 0)
    wide_pos = jnp.concatenate([jnp.full((reach,), -1, jnp.int32), relaid_pos], 0)
    wide_doc = doc_index(lengths, wide_pos)
    result, log_sum_exp, moved_qgrad, wide_kgrad, wide_vgrad = attend(
        moved_query, wide_key, wide_value, moved_grad, relaid_pos, relaid_doc, wide_pos, wide_doc
    )
    moved_kgrad = wide_kgrad[reach:].astype(jnp.bfloat16)
    moved_vgrad = wide_vgrad[reach:].astype(jnp.bfloat16)
    back = jnp.concatenate([result, moved_qgrad, moved_kgrad, moved_vgrad], axis=1).reshape(
        blocks, -1
    )
    returning = jnp.concatenate(
        [select_rows(jnp.transpose(from_prev), back), select_rows(jnp.transpose(from_next), back)],
        0,
    ).astype(jnp.bfloat16)
    came = padded(returning, (("ctx", 0),), spare)
    home = (
        select_rows(jnp.transpose(keep_table), back)
        + select_rows(jnp.transpose(to_prev), came[:spare])
        + select_rows(jnp.transpose(to_next), came[3 * spare :])
    )
    home = home.astype(jnp.bfloat16).reshape(tok_rows, -1)
    attention_out = home[:, :query_width]
    query_grad = home[:, query_width : 2 * query_width]
    key_grad = home[:, 2 * query_width : 2 * query_width + key_width]
    value_grad = home[:, 2 * query_width + key_width :]
    grad_input = project(query_grad, key_grad, value_grad, weight)
    return (attention_out, grad_input, log_sum_exp)


def solution(mesh):
    in_specs = (
        P("ctx", "tp"),
        P("ctx", "tp"),
        P("ctx", "tp"),
        P("ctx", "tp"),
        P(None, "tp"),
        P(),
        P(),
    )
    out_specs = (P("ctx", "tp"), P("ctx", "tp"), P("tp", "ctx"))
    return jax.shard_map(body, mesh=mesh, in_specs=in_specs, out_specs=out_specs, check_vma=False)
```

profile of v0, /device:TPU:128, one launch (start us, length us, event | category | flops | bytes accessed | tf_op | source)
XLA Modules:
  0.0 174.4 jit_solution(1922697924992099666)
XLA Ops:
  7.2 1.4 pad_maximum_fusion
  9.9 1.9 %convolution_convert_fusion.2 = bf16[3,163840]{1,0:T(4,128)(2,1)} fusion(bf16[4,163840]{1,0:T(4,128)(2,1)S(1)} %reshape.332, s32[4]{0:T(128)S(1)} %bitcast_subtract_fusion.1, pred[4]{0:T(512)(128)(4,1)S(1)} %get-tuple-element.58), kind=kOutput, calls=%fused_computation.8 | convolution fusion | flops 4423704 | bytes 2293780 | tf_op jit(solution)/shard_map/dot_general | solution.py:34
  11.8 4.3 %collective-permute-start.1 = (bf16[3,163840]{1,0:T(4,128)(2,1)}, bf16[3,163840]{1,0:T(4,128)(2,1)S(1)}, u32[]{:S(2)}, u32[]{:S(2)}) collective-permute-start(bf16[3,163840]{1,0:T(4,128)(2,1)} %convolution_convert_fusion.2), channel_id=1, source_target_pairs={{8,0},{16,8},{24,16},{32,24},{40,32},{48,40},{56,48},{64,56},{72,6... | collective-permute-start | bytes 2949128 | tf_op jit(solution)/shard_map/ppermute | solution.py:21
  16.4 1.9 %convolution_convert_fusion.3 = bf16[3,163840]{1,0:T(4,128)(2,1)} fusion(bf16[4,163840]{1,0:T(4,128)(2,1)S(1)} %reshape.332, s32[4]{0:T(128)S(1)} %bitcast_subtract_fusion.2, pred[4]{0:T(512)(128)(4,1)S(1)} %get-tuple-element.33), kind=kOutput, calls=%fused_computation.9 | convolution fusion | flops 4423704 | bytes 2293780 | tf_op jit(solution)/shard_map/dot_general | solution.py:34
  18.3 2.1 %collective-permute-start = (bf16[3,163840]{1,0:T(4,128)(2,1)}, bf16[3,163840]{1,0:T(4,128)(2,1)}, u32[]{:S(2)}, u32[]{:S(2)}) collective-permute-start(bf16[3,163840]{1,0:T(4,128)(2,1)} %convolution_convert_fusion.3), channel_id=1, source_target_pairs={{0,8},{8,16},{16,24},{24,32},{32,40},{40,48},{48,56},{56,64},{64,7... | collective-permute-start | bytes 2949128 | tf_op jit(solution)/shard_map/ppermute | solution.py:19
  23.5 21.1 %collective-permute-done.1 = bf16[3,163840]{1,0:T(4,128)(2,1)S(1)} collective-permute-done((bf16[3,163840]{1,0:T(4,128)(2,1)}, bf16[3,163840]{1,0:T(4,128)(2,1)S(1)}, u32[]{:S(2)}, u32[]{:S(2)}) %collective-permute-start.1) | collective-permute-done | bytes 983072 | tf_op jit(solution)/shard_map/ppermute | solution.py:21
  45.5 8.6 %collective-permute-done = bf16[3,163840]{1,0:T(4,128)(2,1)} collective-permute-done((bf16[3,163840]{1,0:T(4,128)(2,1)}, bf16[3,163840]{1,0:T(4,128)(2,1)}, u32[]{:S(2)}, u32[]{:S(2)}) %collective-permute-start) | collective-permute-done | bytes 983072 | tf_op jit(solution)/shard_map/ppermute | solution.py:19
  54.0 2.5 %fusion.1 = bf16[4,163840]{1,0:T(4,128)(2,1)S(1)} fusion(f32[4,163840]{1,0:T(4,128)S(1)} %fusion.58, f32[4,163840]{1,0:T(4,128)S(1)} %fusion.53, bf16[3,163840]{1,0:T(4,128)(2,1)} %collective-permute-done, s32[4]{0:T(128)S(1)} %convert_reduce_fusion.2, pred[4]{0:T(512)(128)(4,1)S(1)} %get-tuple-element.31), kind=kOutput, calls=%fused_computation.4 | convolution fusion | flops 5898264 | bytes 7536660 | tf_op jit(solution)/shard_map/dot_general | solution.py:34
  58.8 2.0 %copy.66 = bf16[512,512]{0,1:T(8,128)(2,1)} copy(bf16[512,512]{1,0:T(8,128)(2,1)} %get-tuple-element.40) | data formatting | bytes 1048576 | tf_op jit(solution)/shard_map/reshape.43
  61.0 1.3 copy.65
  63.6 1.4 fusion.7
  65.0 2.1 %fusion.26 = bf16[768,1,128]{0,2,1:T(8,128)(2,1)S(1)} fusion(bf16[512,4,128]{0,2,1:T(8,128)(2,1)S(1)} %bitcast.146, f32[4,512]{1,0:T(4,128)S(1)} %fusion.7, f32[4,512]{1,0:T(4,128)S(1)} %get-tuple-element.64, f32[768,512,4]{1,0,2:T(8,128)S(1)} %get-tuple-element.65, pred[512,768]{0,1:T(8,128)(4,1)S(1)} %and_and_fusion), kind=kOutput, calls=%fused_computation.36 | convolution fusion | flops 410615808 | bytes 7421952 | tf_op jit(solution)/shard_map/while/body/eval_jaxpr/gjqk,qgjd->kgd/dot_general | solution.py:91
  67.0 2.1 %multiply_reduce_fusion = (f32[512,4]{0,1:T(4,128)S(1)}, bf16[128,4,512]{2,0,1:T(8,128)(2,1)S(1)}) fusion(f32[512,1,4,128]{0,3,2,1:T(8,128)S(1)} %bitcast.144, f32[4,512]{1,0:T(4,128)S(1)} %fusion.7, f32[4,512]{1,0:T(4,128)S(1)} %get-tuple-element.64, f32[768,512,4]{1,0,2:T(8,128)S(1)} %get-tuple-element.65, pred[512,768]{0,1:T(8,128)(4,1)S(1)} %and_and_fusion, ...), kind=kOutput, calls=%fused_computation.38 | convolution fusion | flops 411564032 | bytes 8413184 | tf_op jit(solution)/shard_map/while/body/eval_jaxpr/gjqk,kgd->qgjd/dot_general | solution.py:75
  69.2 3.1 %fusion.10 = bf16[4,512,768]{1,2,0:T(8,128)(2,1)S(1)} fusion(f32[4,512]{1,0:T(4,128)S(1)} %bitcast.152, f32[4,512]{1,0:T(4,128)S(1)} %fusion.7, f32[4,512]{1,0:T(4,128)S(1)} %get-tuple-element.64, f32[768,512,4]{1,0,2:T(8,128)S(1)} %get-tuple-element.65, pred[512,768]{0,1:T(8,128)(4,1)S(1)} %and_and_fusion, bf16[512,4,128]{0,2,1:T(8,128)(2,1)S(1)} %bitcast.147, ...), kind=kOutput, calls=%fused_computation.21 | convolution fusion | flops 415236096 | bytes 10510336 | tf_op jit(solution)/shard_map/while/body/eval_jaxpr/qgjd,kgd->gjqk/dot_general | solution.py:79
  75.9 1.4 convolution_convert_fusion.1
  77.3 1.9 %collective-permute-start.2 = (bf16[3,163840]{1,0:T(4,128)(2,1)S(1)}, bf16[3,163840]{1,0:T(4,128)(2,1)S(1)}, u32[]{:S(2)}, u32[]{:S(2)}) collective-permute-start(bf16[3,163840]{1,0:T(4,128)(2,1)S(1)} %convolution_convert_fusion.1), channel_id=1, source_target_pairs={{0,8},{8,16},{16,24},{24,32},{32,40},{40,48},{48,56},{56,64},{64,7... | collective-permute-start | bytes 2949128 | tf_op jit(solution)/shard_map/ppermute | solution.py:19
  79.2 1.4 convolution_convert_fusion
  80.6 7.2 %collective-permute-start.3 = (bf16[3,163840]{1,0:T(4,128)(2,1)S(1)}, bf16[3,163840]{1,0:T(4,128)(2,1)S(1)}, u32[]{:S(2)}, u32[]{:S(2)}) collective-permute-start(bf16[3,163840]{1,0:T(4,128)(2,1)S(1)} %convolution_convert_fusion), channel_id=1, source_target_pairs={{8,0},{16,8},{24,16},{32,24},{40,32},{48,40},{56,48},{64,56},{72,6... | collective-permute-start | bytes 2949128 | tf_op jit(solution)/shard_map/ppermute | solution.py:21
  87.9 1.4 fusion.51
  89.3 22.6 %collective-permute-done.2 = bf16[3,163840]{1,0:T(4,128)(2,1)S(1)} collective-permute-done((bf16[3,163840]{1,0:T(4,128)(2,1)S(1)}, bf16[3,163840]{1,0:T(4,128)(2,1)S(1)}, u32[]{:S(2)}, u32[]{:S(2)}) %collective-permute-start.2) | collective-permute-done | bytes 983072 | tf_op jit(solution)/shard_map/ppermute | solution.py:19
  111.8 1.3 convolution_add_fusion.1
  114.4 1.4 fusion.2
  117.1 7.8 %fusion.8 = bf16[4096,512]{0,1:T(8,128)(2,1)} fusion(bf16[4096,768]{1,0:T(8,128)(2,1)} %param.11, bf16[512,1280]{1,0:T(8,128)(2,1)S(1)} %reshape.345), kind=kOutput, calls=%fused_computation.19 | convolution fusion | flops 3223322624 | bytes 11272192 | tf_op jit(solution)/shard_map/dot_general | solution.py:121
  126.3 41.3 %reduce-scatter.2.cloned.1.call-done = bf16[512,512]{0,1:T(8,128)(2,1)} async-done(((bf16[4096,512]{0,1:T(8,128)(2,1)}), bf16[512,512]{0,1:T(8,128)(2,1)}) %reduce-scatter.2.cloned.1.call-update) | async-done | bytes 524304 | tf_op jit(solution)/shard_map/reduce_scatter | solution.py:120
  (76 shorter events, 16.5 us)
Async XLA Ops:
  7.2 160.4 %reduce-scatter.2.cloned.1.call-start = ((), (), s32[]{:S(2)}) async-start(), calls=%async_computation.1 | async-start | bytes 4718592 | tf_op jit(solution)/shard_map/reduce_scatter | solution.py:120
  7.2 2.4 %copy-start.2 = (s32[128]{0:T(128)S(1)}, s32[128]{0:T(128)}, u32[]{:S(2)}) copy-start(s32[128]{0:T(128)} %param.13) | copy-start | bytes 1540
  9.7 8.5 %copy-start.3 = (pred[4]{0:T(512)(128)(4,1)}, pred[4]{0:T(512)(128)(4,1)S(1)}, u32[]{:S(2)}) copy-start(pred[4]{0:T(512)(128)(4,1)S(1)} %get-tuple-element.33) | copy-start | bytes 16
  9.7 8.5 %copy-start.5 = (pred[4]{0:T(512)(128)(4,1)}, pred[4]{0:T(512)(128)(4,1)S(1)}, u32[]{:S(2)}) copy-start(pred[4]{0:T(512)(128)(4,1)S(1)} %get-tuple-element.58) | copy-start | bytes 16
  9.9 8.3 %copy-start.9 = (s32[4]{0:T(128)}, s32[4]{0:T(128)S(1)}, u32[]{:S(2)}) copy-start(s32[4]{0:T(128)S(1)} %bitcast_subtract_fusion.1) | copy-start | bytes 52
  11.8 9.2 %copy-start.13 = (s32[64]{0:T(128)S(1)}, s32[64]{0:T(128)}, u32[]{:S(2)}) copy-start(s32[64]{0:T(128)} %param.12) | copy-start | bytes 772
  11.8 32.7 %collective-permute-start.1 = (bf16[3,163840]{1,0:T(4,128)(2,1)}, bf16[3,163840]{1,0:T(4,128)(2,1)S(1)}, u32[]{:S(2)}, u32[]{:S(2)}) collective-permute-start(bf16[3,163840]{1,0:T(4,128)(2,1)} %convolution_convert_fusion.2), channel_id=1, source_target_pairs={{8,0},{16,8},{24,16},{32,24},{40,32},{48,40},{56,48},{64,56},{72,6... | collective-permute-start | bytes 2949128 | tf_op jit(solution)/shard_map/ppermute | solution.py:21
  16.4 4.0 %copy-start.11 = (s32[4]{0:T(128)}, s32[4]{0:T(128)S(1)}, u32[]{:S(2)}) copy-start(s32[4]{0:T(128)S(1)} %bitcast_subtract_fusion.2) | copy-start | bytes 52
  18.3 35.8 %collective-permute-start = (bf16[3,163840]{1,0:T(4,128)(2,1)}, bf16[3,163840]{1,0:T(4,128)(2,1)}, u32[]{:S(2)}, u32[]{:S(2)}) collective-permute-start(bf16[3,163840]{1,0:T(4,128)(2,1)} %convolution_convert_fusion.3), channel_id=1, source_target_pairs={{0,8},{8,16},{16,24},{24,32},{32,40},{40,48},{48,56},{56,64},{64,7... | collective-permute-start | bytes 2949128 | tf_op jit(solution)/shard_map/ppermute | solution.py:19
  21.0 2.5 %copy-start.7 = (s32[4]{0:T(128)}, s32[4]{0:T(128)S(1)}, u32[]{:S(2)}) copy-start(s32[4]{0:T(128)S(1)} %get-tuple-element.57) | copy-start | bytes 52
  63.5 1.4 copy-start.1
  64.9 2.1 %copy-start = (f32[512,512]{0,1:T(8,128)S(1)}, f32[512,512]{0,1:T(8,128)}, u32[]{:S(2)}) copy-start(f32[512,512]{0,1:T(8,128)} %copy.65) | copy-start | bytes 3145732
  75.9 12.0 %copy-start.8 = (s32[4]{0:T(128)S(1)}, s32[4]{0:T(128)}, u32[]{:S(2)}) copy-start(s32[4]{0:T(128)} %copy-done.7) | copy-start | bytes 52
  77.3 34.5 %collective-permute-start.2 = (bf16[3,163840]{1,0:T(4,128)(2,1)S(1)}, bf16[3,163840]{1,0:T(4,128)(2,1)S(1)}, u32[]{:S(2)}, u32[]{:S(2)}) collective-permute-start(bf16[3,163840]{1,0:T(4,128)(2,1)S(1)} %convolution_convert_fusion.1), channel_id=1, source_target_pairs={{0,8},{8,16},{16,24},{24,32},{32,40},{40,48},{48,56},{56,64},{64,7... | collective-permute-start | bytes 2949128 | tf_op jit(solution)/shard_map/ppermute | solution.py:19
  80.6 31.2 %copy-start.6 = (pred[4]{0:T(512)(128)(4,1)S(1)}, pred[4]{0:T(512)(128)(4,1)}, u32[]{:S(2)}) copy-start(pred[4]{0:T(512)(128)(4,1)} %copy-done.5) | copy-start | bytes 16
  80.6 31.2 %copy-start.10 = (s32[4]{0:T(128)S(1)}, s32[4]{0:T(128)}, u32[]{:S(2)}) copy-start(s32[4]{0:T(128)} %copy-done.9) | copy-start | bytes 52
  80.6 33.8 %collective-permute-start.3 = (bf16[3,163840]{1,0:T(4,128)(2,1)S(1)}, bf16[3,163840]{1,0:T(4,128)(2,1)S(1)}, u32[]{:S(2)}, u32[]{:S(2)}) collective-permute-start(bf16[3,163840]{1,0:T(4,128)(2,1)S(1)} %convolution_convert_fusion), channel_id=1, source_target_pairs={{8,0},{16,8},{24,16},{32,24},{40,32},{48,40},{56,48},{64,56},{72,6... | collective-permute-start | bytes 2949128 | tf_op jit(solution)/shard_map/ppermute | solution.py:21
  89.2 25.2 %copy-start.4 = (pred[4]{0:T(512)(128)(4,1)S(1)}, pred[4]{0:T(512)(128)(4,1)}, u32[]{:S(2)}) copy-start(pred[4]{0:T(512)(128)(4,1)} %copy-done.3) | copy-start | bytes 16
  89.2 25.2 %copy-start.12 = (s32[4]{0:T(128)S(1)}, s32[4]{0:T(128)}, u32[]{:S(2)}) copy-start(s32[4]{0:T(128)} %copy-done.11) | copy-start | bytes 52
Sparse Core Ops, SparseCore 0:
  125.0 42.5 reduce-scatter.1
where the time goes:
time: 176 us; the launch traced here: 174 us
  waiting for transfers between devices  94.8 us (54%)
  matrix products  32.9 us (19%)
  starting transfers between devices  15.6 us (9%)
  between operations  14.4 us (8%)
  local copies, waits for them, and re-layouts  9.8 us (6%)
  other arithmetic  6.82 us (4%)
    reduce_scatter x1, waiting for transfers between devices, project(): lax.psum_scatter(lax.dot_general(weight, stacked, (((1,), (1,)), ((), ())...  41.3 us
    ppermute x2, waiting for transfers between devices, padded(): lax.ppermute(tail, axis, [(i, (i + 1) % count) for i in range(ends)])  31.1 us
    ppermute x2, waiting for transfers between devices, padded(): lax.ppermute(head, axis, [((i + 1) % count, i) for i in range(ends)])  22.4 us
    dot_general x10, matrix products, select_rows(): jnp.dot(table.astype(rows.dtype), rows, preferred_element_type=jnp.float3...  14.9 us
    ppermute x2, starting transfers between devices, padded(): lax.ppermute(head, axis, [((i + 1) % count, i) for i in range(ends)])  11.6 us
    dot_general x1, matrix products, project(): lax.dot_general(weight, stacked, (((1,), (1,)), ((), ())), preferred_elem...  7.77 us
    ppermute x2, starting transfers between devices, padded(): lax.ppermute(tail, axis, [(i, (i + 1) % count) for i in range(ends)])  4.02 us
  transfers between devices with their start and end apart: 5, of which 5 were waited for; matrix products, arithmetic and copies ran while one was open for 7% of the time, Pallas kernels for 0%

commit v1 on v0

v1 whole, which is shorter than its diff:
```python
import jax
import jax.numpy as jnp
from jax import lax
from jax.experimental import pallas as pl
from jax.experimental.pallas import tpu as pltpu
from jax.sharding import PartitionSpec as P

HEAD_DIM = 128
BLOCK = 128
GROUP = 4
BLOCKS = 4
REACH_BLOCKS = 2
NEG = -1e30
LOG2E = 1.4426950408889634
MESH = pl.DeviceIdType.MESH
F32 = jnp.float32
BF16 = jnp.bfloat16


def dot(a, b, dims):
    return lax.dot_general(a, b, (dims, ((), ())), preferred_element_type=F32)


def remote(src, dst, send, recv, device):
    return pltpu.make_async_remote_copy(
        src_ref=src,
        dst_ref=dst,
        send_sem=send,
        recv_sem=recv,
        device_id=device,
        device_id_type=MESH,
    )


def kernel(
    q_ref, k_ref, v_ref, g_ref, w_ref, len_ref, plan_ref,
    o_ref, gi_ref, lse_ref,
    kbuf, vbuf, qbuf, gbuf, wown, wpar, dkv, ret, st,
    s2, sp, sm, hp, hm, rp, rm, own, mp, mm,
    obuf, gibuf, lbuf, lout,
    lsem, wsem, osem,
    halo_s, halo_r, w_s, w_r, st_s, st_r, ret_s, ret_r, lse_s, lse_r, rs_s, rs_r,
):
    n_ctx = lax.axis_size("ctx")
    n_tp = lax.axis_size("tp")
    n_y = n_tp // 2
    ctx = lax.axis_index("ctx")
    tp = lax.axis_index("tp")
    y = tp // 2
    core = tp - 2 * y
    nxt = {"ctx": lax.rem(ctx + 1, n_ctx)}
    prv = {"ctx": lax.rem(ctx + n_ctx - 1, n_ctx)}
    par = {"tp": tp + 1 - 2 * core}
    up = {"tp": lax.rem(tp + 2, n_tp)}
    dn = {"tp": lax.rem(tp + n_tp - 2, n_tp)}

    barrier = pltpu.get_barrier_semaphore()
    for device in (nxt, prv, par, up, dn):
        pl.semaphore_signal(barrier, inc=1, device_id=device, device_id_type=MESH)

    locals_ = [
        pltpu.make_async_copy(k_ref, kbuf.at[pl.ds(256, 512)], lsem.at[0]),
        pltpu.make_async_copy(q_ref, qbuf, lsem.at[1]),
        pltpu.make_async_copy(v_ref, vbuf.at[pl.ds(256, 512)], lsem.at[2]),
        pltpu.make_async_copy(g_ref, gbuf, lsem.at[3]),
    ]
    for copy in locals_:
        copy.start()

    def w_rows(r, c):
        return pl.ds(pl.multiple_of((2 * lax.rem(y + r, n_y) + c) * 512, 512), 512)

    w_local = [
        pltpu.make_async_copy(w_ref.at[w_rows(r, core)], wown.at[r], wsem.at[r])
        for r in range(4)
    ]
    for r in (2, 1, 3, 0):
        w_local[r].start()

    first = ctx * BLOCKS

    def scan_lengths(i, carry):
        total = carry[0] + len_ref[i]
        return (total,) + tuple(
            carry[1 + b] + jnp.where(total == (first + b - 1) * BLOCK, 1, 0)
            for b in range(5)
        )

    start = jnp.int32(0)
    edge = jnp.where(ctx == 0, 1, 0).astype(jnp.int32)
    found = lax.fori_loop(
        0, len_ref.shape[0], scan_lengths, (start, start, edge, start, start, start)
    )[1:]

    pl.semaphore_wait(barrier, 5)

    halo = {}
    slot = 0
    for b in (1, 0):
        for src, dst in ((k_ref, kbuf), (v_ref, vbuf)):
            copy = remote(
                src.at[pl.ds(256 + b * BLOCK, BLOCK)],
                dst.at[pl.ds(b * BLOCK, BLOCK)],
                halo_s.at[slot], halo_r.at[slot], nxt,
            )
            copy.start()
            halo.setdefault(b, []).append(copy)
            slot += 1
    w_swap = [
        remote(w_ref.at[w_rows(r, 1 - core)], wpar.at[r], w_s.at[r], w_r.at[r], par)
        for r in range(4)
    ]
    for r in (2, 1, 3, 0):
        w_swap[r].start()

    for copy in locals_:
        copy.wait()

    scale = HEAD_DIM ** -0.5
    causal = lax.broadcasted_iota(jnp.int32, (BLOCK, BLOCK), 0) <= lax.broadcasted_iota(
        jnp.int32, (BLOCK, BLOCK), 1
    )
    causal_bias = jnp.where(causal, 0.0, NEG).astype(F32)
    causal_bias = jnp.concatenate([causal_bias] * GROUP, axis=1)
    written = set()

    def add_grad(which, index, value):
        rows = pl.ds(index * BLOCK, BLOCK)
        if (which, index) in written:
            dkv[which, rows, :] += value
        else:
            written.add((which, index))
            dkv[which, rows, :] = value

    def heads_in_rows(ref, qb):
        rows = pl.ds(qb * BLOCK, BLOCK)
        return jnp.concatenate(
            [ref[rows, pl.ds(h * HEAD_DIM, HEAD_DIM)] for h in range(GROUP)], axis=0
        )

    def attend(qb):
        rows = pl.ds(qb * BLOCK, BLOCK)
        keys = kbuf[pl.ds(qb * BLOCK, 3 * BLOCK), :]
        vals = vbuf[pl.ds(qb * BLOCK, 3 * BLOCK), :]
        queries = heads_in_rows(qbuf, qb)
        grads = heads_in_rows(gbuf, qb)
        near = jnp.where(found[qb + 1] > 0, NEG, 0.0).astype(F32)
        far = jnp.where(found[qb + 1] + found[qb] > 0, NEG, 0.0).astype(F32)
        scores = dot(keys, queries, ((1,), (1,)))
        prob = dot(vals, grads, ((1,), (1,)))
        scores = jnp.concatenate(
            [
                scores[:BLOCK] + far,
                scores[BLOCK : 2 * BLOCK] + near,
                scores[2 * BLOCK :] + causal_bias,
            ],
            axis=0,
        )
        top = jnp.max(scores, axis=0, keepdims=True)
        raised = jnp.exp2((scores - top) * (scale * LOG2E))
        total = jnp.sum(raised, axis=0, keepdims=True)
        mixed = jnp.sum(raised * prob, axis=0, keepdims=True)
        inverse = 1.0 / total
        row_dot = mixed * inverse
        lse = top * scale + jnp.log(total)
        for h in range(GROUP):
            lbuf[0, pl.ds(h, 1), rows] = lse[:, h * BLOCK : (h + 1) * BLOCK]
        weights = raised * inverse
        weights_low = weights.astype(BF16)
        score_grad = (weights * (prob - row_dot)).astype(BF16)
        out = dot(vals, weights_low, ((0,), (0,))).astype(BF16)
        query_grad = (dot(keys, score_grad, ((0,), (0,))) * scale).astype(BF16)
        for h in range(GROUP):
            columns = slice(h * BLOCK, (h + 1) * BLOCK)
            obuf[rows, pl.ds(h * HEAD_DIM, HEAD_DIM)] = out[:, columns].T
            st[0, qb, :, pl.ds(h * HEAD_DIM, HEAD_DIM)] = query_grad[:, columns].T
        key_add = dot(score_grad, queries, ((1,), (0,)))
        value_add = dot(weights_low, grads, ((1,), (0,)))
        for b in range(3):
            part = slice(b * BLOCK, (b + 1) * BLOCK)
            add_grad(0, qb + b, key_add[part])
            add_grad(1, qb + b, value_add[part])

    st_swap = [
        remote(st.at[0, t], st.at[1, t], st_s.at[t], st_r.at[t], par) for t in range(BLOCKS)
    ]

    def finish_tokens(t):
        rows = pl.ds((t + REACH_BLOCKS) * BLOCK, BLOCK)
        key_grad = dkv[0, rows, :]
        value_grad = dkv[1, rows, :]
        if t >= 2:
            back = pl.ds((t - 2) * BLOCK, BLOCK)
            key_grad = key_grad + ret[0, back, :]
            value_grad = value_grad + ret[1, back, :]
        st[0, t, :, pl.ds(GROUP * HEAD_DIM, HEAD_DIM)] = (key_grad * scale).astype(BF16)
        st[0, t, :, pl.ds((GROUP + 1) * HEAD_DIM, HEAD_DIM)] = value_grad.astype(BF16)
        st_swap[t].start()

    attend(2)
    attend(3)
    for copy in halo[1]:
        copy.wait_recv()
    attend(1)
    finish_tokens(1)
    for copy in halo[0]:
        copy.wait_recv()
    attend(0)
    finish_tokens(0)

    back_copy = remote(dkv.at[:, pl.ds(0, 256), :], ret, ret_s, ret_r, prv)
    back_copy.start()
    lse_next = remote(lbuf.at[0], lbuf.at[1], lse_s.at[0], lse_r.at[0], nxt)
    lse_prev = remote(lbuf.at[0], lbuf.at[2], lse_s.at[1], lse_r.at[1], prv)
    lse_next.start()
    lse_prev.start()
    out_copy = pltpu.make_async_copy(obuf, o_ref, osem.at[0])
    out_copy.start()

    HALF = BLOCK // 2
    lo, hi = pl.ds(0, HALF), pl.ds(HALF, HALF)
    for r in range(4):
        w_local[r].wait()

    sends = {}
    for t in range(BLOCKS):
        sends[t] = dict(
            h_up=remote(s2.at[t, lo], hp.at[t], rs_s.at[t, 0], rs_r.at[t, 0], up),
            h_dn=remote(s2.at[t, hi], hm.at[t], rs_s.at[t, 1], rs_r.at[t, 1], dn),
            u_up=remote(sp.at[t, hi], rp.at[t, hi], rs_s.at[t, 2], rs_r.at[t, 2], up),
            u_dn=remote(sm.at[t, lo], rm.at[t, lo], rs_s.at[t, 3], rs_r.at[t, 3], dn),
            m_up=remote(sp.at[t, lo], rp.at[t, lo], rs_s.at[t, 4], rs_r.at[t, 4], up),
            m_dn=remote(sm.at[t, hi], rm.at[t, hi], rs_s.at[t, 5], rs_r.at[t, 5], dn),
        )

    def project(t, first_time):
        st_swap[t].wait_recv()

        def part(r):
            if first_time:
                w_swap[r].wait_recv()
            return dot(st[0, t], wown[r], ((1,), (1,))) + dot(st[1, t], wpar[r], ((1,), (1,)))

        s2[t] = part(2).astype(BF16)
        sends[t]["h_up"].start()
        sends[t]["h_dn"].start()
        piece = part(1)
        sp[t, hi, :] = piece[HALF:].astype(BF16)
        sends[t]["u_up"].start()
        mp[t] = piece[:HALF]
        piece = part(3)
        sm[t, lo, :] = piece[:HALF].astype(BF16)
        sends[t]["u_dn"].start()
        mm[t] = piece[HALF:]
        own[t] = part(0)

    def merge(t):
        sends[t]["h_up"].wait_recv()
        sp[t, lo, :] = (mp[t] + hp[t].astype(F32)).astype(BF16)
        sends[t]["m_up"].start()
        sends[t]["h_dn"].wait_recv()
        sm[t, hi, :] = (mm[t] + hm[t].astype(F32)).astype(BF16)
        sends[t]["m_dn"].start()

    gi_copies = []

    def finish(t):
        for name in ("u_up", "u_dn", "m_up", "m_dn"):
            sends[t][name].wait_recv()
        rows = pl.ds(t * BLOCK, BLOCK)
        gibuf[rows, :] = (own[t] + rp[t].astype(F32) + rm[t].astype(F32)).astype(BF16)
        copy = pltpu.make_async_copy(gibuf.at[rows], gi_ref.at[rows], osem.at[1 + t])
        copy.start()
        gi_copies.append(copy)

    project(1, True)
    project(0, False)
    back_copy.wait_recv()
    finish_tokens(2)
    finish_tokens(3)
    merge(1)
    project(2, False)
    merge(0)
    project(3, False)
    merge(2)

    lse_next.wait_recv()
    lse_prev.wait_recv()
    picked = [jnp.zeros((GROUP, BLOCK), F32) for _ in range(BLOCKS)]
    rank = jnp.int32(0)
    for source, device in ((1, prv["ctx"]), (0, ctx), (2, nxt["ctx"])):
        for b in range(BLOCKS):
            hit = jnp.where(plan_ref[device * BLOCKS + b] == ctx, 1, 0)
            piece = lbuf[source, :, pl.ds(b * BLOCK, BLOCK)]
            for s in range(BLOCKS):
                take = jnp.where((hit == 1) & (rank == s), 1.0, 0.0).astype(F32)
                picked[s] = picked[s] + piece * take
            rank = rank + hit
    for s in range(BLOCKS):
        lout[:, pl.ds(s * BLOCK, BLOCK)] = picked[s]
    lse_copy = pltpu.make_async_copy(lout, lse_ref, osem.at[5])
    lse_copy.start()

    merge(3)
    for t in (1, 0, 2, 3):
        finish(t)

    out_copy.wait()
    lse_copy.wait()
    for copy in gi_copies:
        copy.wait()
    for b in (1, 0):
        for copy in halo[b]:
            copy.wait_send()
    for copy in w_swap:
        copy.wait_send()
    for copy in st_swap:
        copy.wait_send()
    back_copy.wait_send()
    lse_next.wait_send()
    lse_prev.wait_send()
    for t in range(BLOCKS):
        for copy in sends[t].values():
            copy.wait_send()


def body(queries, key_states, values, out_grad, weight, lengths, block_plan):
    anywhere = pl.BlockSpec(memory_space=pl.ANY)
    scalars = pl.BlockSpec(memory_space=pltpu.SMEM)
    dma = pltpu.SemaphoreType.DMA
    return pl.pallas_call(
        kernel,
        out_shape=(
            jax.ShapeDtypeStruct((512, 512), BF16),
            jax.ShapeDtypeStruct((512, 512), BF16),
            jax.ShapeDtypeStruct((GROUP, 512), F32),
        ),
        in_specs=[anywhere] * 5 + [scalars] * 2,
        out_specs=(anywhere,) * 3,
        scratch_shapes=[
            pltpu.VMEM((768, 128), BF16),
            pltpu.VMEM((768, 128), BF16),
            pltpu.VMEM((512, 512), BF16),
            pltpu.VMEM((512, 512), BF16),
            pltpu.VMEM((4, 512, 768), BF16),
            pltpu.VMEM((4, 512, 768), BF16),
            pltpu.VMEM((2, 768, 128), F32),
            pltpu.VMEM((2, 256, 128), F32),
            pltpu.VMEM((2, 4, 128, 768), BF16),
            pltpu.VMEM((4, 128, 512), BF16),
            pltpu.VMEM((4, 128, 512), BF16),
            pltpu.VMEM((4, 128, 512), BF16),
            pltpu.VMEM((4, 64, 512), BF16),
            pltpu.VMEM((4, 64, 512), BF16),
            pltpu.VMEM((4, 128, 512), BF16),
            pltpu.VMEM((4, 128, 512), BF16),
            pltpu.VMEM((4, 128, 512), F32),
            pltpu.VMEM((4, 64, 512), F32),
            pltpu.VMEM((4, 64, 512), F32),
            pltpu.VMEM((512, 512), BF16),
            pltpu.VMEM((512, 512), BF16),
            pltpu.VMEM((3, GROUP, 512), F32),
            pltpu.VMEM((GROUP, 512), F32),
            dma((4,)),
            dma((4,)),
            dma((6,)),
            dma((4,)), dma((4,)),
            dma((4,)), dma((4,)),
            dma((4,)), dma((4,)),
            dma, dma,
            dma((2,)), dma((2,)),
            dma((4, 6)), dma((4, 6)),
        ],
        compiler_params=pltpu.CompilerParams(
            collective_id=0, has_side_effects=True, vmem_limit_bytes=44 * 1024 * 1024
        ),
    )(queries, key_states, values, out_grad, weight, lengths, block_plan)


def solution(mesh):
    in_specs = (
        P("ctx", "tp"),
        P("ctx", "tp"),
        P("ctx", "tp"),
        P("ctx", "tp"),
        P(None, "tp"),
        P(),
        P(),
    )
    out_specs = (P("ctx", "tp"), P("ctx", "tp"), P("tp", "ctx"))
    return jax.shard_map(body, mesh=mesh, in_specs=in_specs, out_specs=out_specs, check_vma=False)
```

time: 176 us -> 50.2 us (0.29)
  the two profiles are of different devices: /device:TPU:128 before, /device:TPU:1 now
where the time goes in v1:
time: 50.2 us; the launch traced here: 50 us
  Pallas kernels  39.1 us (78%)
  local copies, waits for them, and re-layouts  10.2 us (20%)
  between operations  0.66 us (1%)
    pallas_call x1, Pallas kernels, body(): pl.pallas_call(kernel, out_shape=(jax.ShapeDtypeStruct((512, 512), BF16),...  39.1 us
    unnamed x17, local copies, waits for them, and re-layouts  10.2 us

profile of v1, /device:TPU:1, one launch (start us, length us, event | category | flops | bytes accessed | tf_op | source)
XLA Modules:
  0.0 50.0 jit_solution(15490959151878905543)
XLA Ops:
  0.6 0.0 copy-start
  0.6 2.8 %copy-done = bf16[4096,768]{1,0:T(8,128)(2,1)S(1)} copy-done((bf16[4096,768]{1,0:T(8,128)(2,1)S(1)}, bf16[4096,768]{1,0:T(8,128)(2,1)}, u32[]{:S(2)}) %copy-start) | copy-done | bytes 6291480
  3.4 0.0 copy-start.1
  3.4 1.0 %copy-done.1 = bf16[512,512]{1,0:T(8,128)(2,1)S(1)} copy-done((bf16[512,512]{1,0:T(8,128)(2,1)S(1)}, bf16[512,512]{1,0:T(8,128)(2,1)}, u32[]{:S(2)}) %copy-start.1) | copy-done | bytes 524312
  4.5 0.0 copy-start.2
  4.5 1.0 %copy-done.2 = bf16[512,512]{1,0:T(8,128)(2,1)S(1)} copy-done((bf16[512,512]{1,0:T(8,128)(2,1)S(1)}, bf16[512,512]{1,0:T(8,128)(2,1)}, u32[]{:S(2)}) %copy-start.2) | copy-done | bytes 524312
  5.5 0.0 copy-start.3
  5.5 0.9 %copy-done.3 = bf16[512,128]{1,0:T(8,128)(2,1)S(1)} copy-done((bf16[512,128]{1,0:T(8,128)(2,1)S(1)}, bf16[512,128]{1,0:T(8,128)(2,1)}, u32[]{:S(2)}) %copy-start.3) | copy-done | bytes 131096
  6.4 0.0 copy-start.4
  6.4 0.9 %copy-done.4 = bf16[512,128]{1,0:T(8,128)(2,1)S(1)} copy-done((bf16[512,128]{1,0:T(8,128)(2,1)S(1)}, bf16[512,128]{1,0:T(8,128)(2,1)}, u32[]{:S(2)}) %copy-start.4) | copy-done | bytes 131096
  7.3 0.0 copy-start.5
  7.3 0.7 %copy-done.5 = s32[64]{0:T(128)S(1)} copy-done((s32[64]{0:T(128)S(1)}, s32[64]{0:T(128)}, u32[]{:S(2)}) %copy-start.5) | copy-done | bytes 280
  8.0 0.0 copy-start.6
  8.0 0.7 %copy-done.6 = s32[128]{0:T(128)S(1)} copy-done((s32[128]{0:T(128)S(1)}, s32[128]{0:T(128)}, u32[]{:S(2)}) %copy-start.6) | copy-done | bytes 536
  8.6 39.1 %shard_map.94 = (bf16[512,512]{1,0:T(8,128)(2,1)S(1)}, bf16[512,512]{1,0:T(8,128)(2,1)S(1)}, f32[4,512]{1,0:T(4,128)S(1)}) custom-call(bf16[512,512]{1,0:T(8,128)(2,1)S(1)} %copy-done.1, bf16[512,128]{1,0:T(8,128)(2,1)S(1)} %copy-done.3, bf16[512,128]{1,0:T(8,128)(2,1)S(1)} %copy-done.4, bf16[512,512]{1,0:T(8,128)(2,1)S(1)} %copy-done.2, ...), custom_call_target="tpu_custom_call" | custom-call | tf_op jit(solution)/shard_map/pallas_call | solution.py:331
  47.8 0.8 %copy.13 = bf16[512,512]{1,0:T(8,128)(2,1)} copy(bf16[512,512]{1,0:T(8,128)(2,1)S(1)} %get-tuple-element.6) | data formatting | bytes 1048576
  48.6 0.8 %copy.14 = bf16[512,512]{1,0:T(8,128)(2,1)} copy(bf16[512,512]{1,0:T(8,128)(2,1)S(1)} %get-tuple-element.7) | data formatting | bytes 1048576
  49.4 0.6 %copy.15 = f32[4,512]{1,0:T(4,128)} copy(f32[4,512]{1,0:T(4,128)S(1)} %get-tuple-element.8) | data formatting | bytes 16384
Async XLA Ops:
  0.6 2.8 %copy-start = (bf16[4096,768]{1,0:T(8,128)(2,1)S(1)}, bf16[4096,768]{1,0:T(8,128)(2,1)}, u32[]{:S(2)}) copy-start(bf16[4096,768]{1,0:T(8,128)(2,1)} %w_ref.1) | copy-start | bytes 18874372
  3.4 1.0 %copy-start.1 = (bf16[512,512]{1,0:T(8,128)(2,1)S(1)}, bf16[512,512]{1,0:T(8,128)(2,1)}, u32[]{:S(2)}) copy-start(bf16[512,512]{1,0:T(8,128)(2,1)} %q_ref.1) | copy-start | bytes 1572868
  4.5 1.0 %copy-start.2 = (bf16[512,512]{1,0:T(8,128)(2,1)S(1)}, bf16[512,512]{1,0:T(8,128)(2,1)}, u32[]{:S(2)}) copy-start(bf16[512,512]{1,0:T(8,128)(2,1)} %g_ref.1) | copy-start | bytes 1572868
  5.5 0.9 %copy-start.3 = (bf16[512,128]{1,0:T(8,128)(2,1)S(1)}, bf16[512,128]{1,0:T(8,128)(2,1)}, u32[]{:S(2)}) copy-start(bf16[512,128]{1,0:T(8,128)(2,1)} %k_ref.1) | copy-start | bytes 393220
  6.4 0.9 %copy-start.4 = (bf16[512,128]{1,0:T(8,128)(2,1)S(1)}, bf16[512,128]{1,0:T(8,128)(2,1)}, u32[]{:S(2)}) copy-start(bf16[512,128]{1,0:T(8,128)(2,1)} %v_ref.1) | copy-start | bytes 393220
  7.3 0.7 %copy-start.5 = (s32[64]{0:T(128)S(1)}, s32[64]{0:T(128)}, u32[]{:S(2)}) copy-start(s32[64]{0:T(128)} %len_ref.1) | copy-start | bytes 772
  8.0 0.7 %copy-start.6 = (s32[128]{0:T(128)S(1)}, s32[128]{0:T(128)}, u32[]{:S(2)}) copy-start(s32[128]{0:T(128)} %plan_ref.1) | copy-start | bytes 1540

commit v2 on v1

--- a/solution.py
+++ b/solution.py
@@ -11,6 +11,7 @@
 BLOCKS = 4
 REACH_BLOCKS = 2
 NEG = -1e30
+VMEM_LIMIT = 60 * 1024 * 1024
 LOG2E = 1.4426950408889634
 MESH = pl.DeviceIdType.MESH
 F32 = jnp.float32
@@ -33,11 +34,11 @@
 
 
 def kernel(
-    q_ref, k_ref, v_ref, g_ref, w_ref, len_ref, plan_ref,
+    q_ref, k_ref, v_ref, g_ref, w_ref, len_hbm, plan_hbm,
     o_ref, gi_ref, lse_ref,
     kbuf, vbuf, qbuf, gbuf, wown, wpar, dkv, ret, st,
     s2, sp, sm, hp, hm, rp, rm, own, mp, mm,
-    obuf, gibuf, lbuf, lout,
+    obuf, gibuf, lbuf, lout, len_ref, plan_ref,
     lsem, wsem, osem,
     halo_s, halo_r, w_s, w_r, st_s, st_r, ret_s, ret_r, lse_s, lse_r, rs_s, rs_r,
 ):
@@ -54,9 +55,21 @@
     up = {"tp": lax.rem(tp + 2, n_tp)}
     dn = {"tp": lax.rem(tp + n_tp - 2, n_tp)}
 
+    has_next = ctx < n_ctx - 1
+    has_prev = ctx > 0
+
+    def greet(device):
+        pl.semaphore_signal(barrier, inc=1, device_id=device, device_id_type=MESH)
+
     barrier = pltpu.get_barrier_semaphore()
-    for device in (nxt, prv, par, up, dn):
-        pl.semaphore_signal(barrier, inc=1, device_id=device, device_id_type=MESH)
+    pl.when(has_next)(lambda: greet(nxt))
+    pl.when(has_prev)(lambda: greet(prv))
+    for device in (par, up, dn):
+        greet(device)
+    len_copy = pltpu.make_async_copy(len_hbm, len_ref, lsem.at[4])
+    plan_copy = pltpu.make_async_copy(plan_hbm, plan_ref, lsem.at[5])
+    len_copy.start()
+    plan_copy.start()
 
     locals_ = [
         pltpu.make_async_copy(k_ref, kbuf.at[pl.ds(256, 512)], lsem.at[0]),
@@ -77,6 +90,18 @@
     for r in (2, 1, 3, 0):
         w_local[r].start()
 
+    def no_halo():
+        kbuf[pl.ds(0, 256), :] = jnp.zeros((256, 128), BF16)
+        vbuf[pl.ds(0, 256), :] = jnp.zeros((256, 128), BF16)
+        lbuf[1] = jnp.zeros((GROUP, 512), F32)
+
+    def no_return():
+        ret[...] = jnp.zeros((2, 256, 128), F32)
+        lbuf[2] = jnp.zeros((GROUP, 512), F32)
+
+    pl.when(jnp.logical_not(has_prev))(no_halo)
+    pl.when(jnp.logical_not(has_next))(no_return)
+
     first = ctx * BLOCKS
 
     def scan_lengths(i, carry):
@@ -88,11 +113,15 @@
 
     start = jnp.int32(0)
     edge = jnp.where(ctx == 0, 1, 0).astype(jnp.int32)
+    len_copy.wait()
+    plan_copy.wait()
     found = lax.fori_loop(
         0, len_ref.shape[0], scan_lengths, (start, start, edge, start, start, start)
     )[1:]
 
-    pl.semaphore_wait(barrier, 5)
+    pl.semaphore_wait(
+        barrier, 3 + jnp.where(has_next, 1, 0) + jnp.where(has_prev, 1, 0)
+    )
 
     halo = {}
     slot = 0
@@ -103,7 +132,7 @@
                 dst.at[pl.ds(b * BLOCK, BLOCK)],
                 halo_s.at[slot], halo_r.at[slot], nxt,
             )
-            copy.start()
+            pl.when(has_next)(copy.start)
             halo.setdefault(b, []).append(copy)
             slot += 1
     w_swap = [
@@ -200,20 +229,20 @@
     attend(2)
     attend(3)
     for copy in halo[1]:
-        copy.wait_recv()
+        pl.when(has_prev)(copy.wait_recv)
     attend(1)
     finish_tokens(1)
     for copy in halo[0]:
-        copy.wait_recv()
+        pl.when(has_prev)(copy.wait_recv)
     attend(0)
     finish_tokens(0)
 
     back_copy = remote(dkv.at[:, pl.ds(0, 256), :], ret, ret_s, ret_r, prv)
-    back_copy.start()
+    pl.when(has_prev)(back_copy.start)
     lse_next = remote(lbuf.at[0], lbuf.at[1], lse_s.at[0], lse_r.at[0], nxt)
     lse_prev = remote(lbuf.at[0], lbuf.at[2], lse_s.at[1], lse_r.at[1], prv)
-    lse_next.start()
-    lse_prev.start()
+    pl.when(has_next)(lse_next.start)
+    pl.when(has_prev)(lse_prev.start)
     out_copy = pltpu.make_async_copy(obuf, o_ref, osem.at[0])
     out_copy.start()
 
@@ -275,7 +304,7 @@
 
     project(1, True)
     project(0, False)
-    back_copy.wait_recv()
+    pl.when(has_next)(back_copy.wait_recv)
     finish_tokens(2)
     finish_tokens(3)
     merge(1)
@@ -284,13 +313,17 @@
     project(3, False)
     merge(2)
 
-    lse_next.wait_recv()
-    lse_prev.wait_recv()
+    pl.when(has_prev)(lse_next.wait_recv)
+    pl.when(has_next)(lse_prev.wait_recv)
     picked = [jnp.zeros((GROUP, BLOCK), F32) for _ in range(BLOCKS)]
     rank = jnp.int32(0)
-    for source, device in ((1, prv["ctx"]), (0, ctx), (2, nxt["ctx"])):
+    one = jnp.int32(1)
+    before, after = jnp.where(has_prev, 1, 0), jnp.where(has_next, 1, 0)
+    for source, device, valid in (
+        (1, prv["ctx"], before), (0, ctx, one), (2, nxt["ctx"], after),
+    ):
         for b in range(BLOCKS):
-            hit = jnp.where(plan_ref[device * BLOCKS + b] == ctx, 1, 0)
+            hit = jnp.where(plan_ref[device * BLOCKS + b] == ctx, valid, 0)
             piece = lbuf[source, :, pl.ds(b * BLOCK, BLOCK)]
             for s in range(BLOCKS):
                 take = jnp.where((hit == 1) & (rank == s), 1.0, 0.0).astype(F32)
@@ -311,31 +344,43 @@
         copy.wait()
     for b in (1, 0):
         for copy in halo[b]:
-            copy.wait_send()
+            pl.when(has_next)(copy.wait_send)
     for copy in w_swap:
         copy.wait_send()
     for copy in st_swap:
         copy.wait_send()
-    back_copy.wait_send()
-    lse_next.wait_send()
-    lse_prev.wait_send()
+    pl.when(has_prev)(back_copy.wait_send)
+    pl.when(has_next)(lse_next.wait_send)
+    pl.when(has_prev)(lse_prev.wait_send)
     for t in range(BLOCKS):
         for copy in sends[t].values():
             copy.wait_send()
 
 
+def publish(o_ref, gi_ref, lse_ref, o_out, gi_out, lse_out, sems):
+    copies = [pltpu.make_async_copy(lse_ref, lse_out, sems.at[8])]
+    for part in range(4):
+        rows = pl.ds(part * 128, 128)
+        copies.append(pltpu.make_async_copy(gi_ref.at[rows], gi_out.at[rows], sems.at[part]))
+        copies.append(pltpu.make_async_copy(o_ref.at[rows], o_out.at[rows], sems.at[4 + part]))
+    for copy in copies:
+        copy.start()
+    for copy in copies:
+        copy.wait()
+
+
 def body(queries, key_states, values, out_grad, weight, lengths, block_plan):
     anywhere = pl.BlockSpec(memory_space=pl.ANY)
-    scalars = pl.BlockSpec(memory_space=pltpu.SMEM)
     dma = pltpu.SemaphoreType.DMA
-    return pl.pallas_call(
+    shapes = (
+        jax.ShapeDtypeStruct((512, 512), BF16),
+        jax.ShapeDtypeStruct((512, 512), BF16),
+        jax.ShapeDtypeStruct((GROUP, 512), F32),
+    )
+    results = pl.pallas_call(
         kernel,
-        out_shape=(
-            jax.ShapeDtypeStruct((512, 512), BF16),
-            jax.ShapeDtypeStruct((512, 512), BF16),
-            jax.ShapeDtypeStruct((GROUP, 512), F32),
-        ),
-        in_specs=[anywhere] * 5 + [scalars] * 2,
+        out_shape=shapes,
+        in_specs=[anywhere] * 7,
         out_specs=(anywhere,) * 3,
         scratch_shapes=[
             pltpu.VMEM((768, 128), BF16),
@@ -361,7 +406,9 @@
             pltpu.VMEM((512, 512), BF16),
             pltpu.VMEM((3, GROUP, 512), F32),
             pltpu.VMEM((GROUP, 512), F32),
-            dma((4,)),
+            pltpu.SMEM(lengths.shape, jnp.int32),
+            pltpu.SMEM(block_plan.shape, jnp.int32),
+            dma((6,)),
             dma((4,)),
             dma((6,)),
             dma((4,)), dma((4,)),
@@ -372,9 +419,17 @@
             dma((4, 6)), dma((4, 6)),
         ],
         compiler_params=pltpu.CompilerParams(
-            collective_id=0, has_side_effects=True, vmem_limit_bytes=44 * 1024 * 1024
+            collective_id=0, has_side_effects=True, vmem_limit_bytes=VMEM_LIMIT
         ),
     )(queries, key_states, values, out_grad, weight, lengths, block_plan)
+    return pl.pallas_call(
+        publish,
+        out_shape=shapes,
+        in_specs=[anywhere] * 3,
+        out_specs=(anywhere,) * 3,
+        scratch_shapes=[dma((9,))],
+        compiler_params=pltpu.CompilerParams(vmem_limit_bytes=VMEM_LIMIT),
+    )(*results)
 
 
 def solution(mesh):

time: 50.2 us -> 69.3 us (1.38)
  the two profiles are of different devices: /device:TPU:1 before, /device:TPU:103 now
where the time goes in v2:
time: 69.3 us; the launch traced here: 69.2 us
  Pallas kernels  68.5 us (99%)
    pallas_call x1, Pallas kernels, body(): pl.pallas_call(kernel, out_shape=shapes, in_specs=[anywhere] * 7, out_spe...  35.3 us
    pallas_call x1, Pallas kernels, body(): pl.pallas_call(publish, out_shape=shapes, in_specs=[anywhere] * 3, out_sp...  33.2 us

profile of v2, /device:TPU:103, one launch (start us, length us, event | category | flops | bytes accessed | tf_op | source)
XLA Modules:
  0.0 69.2 jit_solution(13035554704088757915)
XLA Ops:
  0.6 35.3 %shard_map.94 = (bf16[512,512]{1,0:T(8,128)(2,1)}, bf16[512,512]{1,0:T(8,128)(2,1)}, f32[4,512]{1,0:T(4,128)}) custom-call(bf16[512,512]{1,0:T(8,128)(2,1)} %q_ref.1, bf16[512,128]{1,0:T(8,128)(2,1)} %k_ref.1, bf16[512,128]{1,0:T(8,128)(2,1)} %v_ref.1, bf16[512,512]{1,0:T(8,128)(2,1)} %g_ref.1, bf16[4096,768]{1,0:T(8,128)(2,1)} %w_ref.1, s32[64]{0:T(128)} %len_hbm.1, ...), custom_call_target="tpu_custom_call" | custom-call | tf_op jit(solution)/shard_map/pallas_call | solution.py:380
  36.0 33.2 %shard_map.95 = (bf16[512,512]{1,0:T(8,128)(2,1)}, bf16[512,512]{1,0:T(8,128)(2,1)}, f32[4,512]{1,0:T(4,128)}) custom-call(bf16[512,512]{1,0:T(8,128)(2,1)} %get-tuple-element.6.o_ref, bf16[512,512]{1,0:T(8,128)(2,1)} %get-tuple-element.7.gi_ref, f32[4,512]{1,0:T(4,128)} %get-tuple-element.8.lse_ref), custom_call_target="tpu_custom_call" | custom-call | tf_op jit(solution)/shard_map/pallas_call | solution.py:425

commit v3 on v2

--- a/solution.py
+++ b/solution.py
@@ -11,7 +11,7 @@
 BLOCKS = 4
 REACH_BLOCKS = 2
 NEG = -1e30
-VMEM_LIMIT = 60 * 1024 * 1024
+VMEM_LIMIT = 40 * 1024 * 1024
 LOG2E = 1.4426950408889634
 MESH = pl.DeviceIdType.MESH
 F32 = jnp.float32
@@ -377,6 +377,10 @@
         jax.ShapeDtypeStruct((512, 512), BF16),
         jax.ShapeDtypeStruct((GROUP, 512), F32),
     )
+    operands = [
+        pltpu.with_memory_space_constraint(operand, pltpu.HBM)
+        for operand in (queries, key_states, values, out_grad, weight, lengths, block_plan)
+    ]
     results = pl.pallas_call(
         kernel,
         out_shape=shapes,
@@ -421,7 +425,7 @@
         compiler_params=pltpu.CompilerParams(
             collective_id=0, has_side_effects=True, vmem_limit_bytes=VMEM_LIMIT
         ),
-    )(queries, key_states, values, out_grad, weight, lengths, block_plan)
+    )(*operands)
     return pl.pallas_call(
         publish,
         out_shape=shapes,

time: 69.3 us -> 36.6 us (0.53)
  Pallas kernels: 68.5 us -> 35.9 us
    pallas_call x1, Pallas kernels: 33.2 us -> 1.04 us  [body(): pl.pallas_call(publish, out_shape=shapes, in_specs=[anywhere] * 3, out_sp...]
where the time goes in v3:
time: 36.6 us
  Pallas kernels  35.9 us (98%)
  between operations  0.64 us (2%)
    pallas_call x1, Pallas kernels, body(): pl.pallas_call(kernel, out_shape=shapes, in_specs=[anywhere] * 7, out_spe...  34.9 us
    pallas_call x1, Pallas kernels, body(): pl.pallas_call(publish, out_shape=shapes, in_specs=[anywhere] * 3, out_sp...  1.04 us

profile of v3, /device:TPU:103, one launch (start us, length us, event | category | flops | bytes accessed | tf_op | source)
XLA Modules:
  0.0 36.6 jit_solution(11237798254532942929)
XLA Ops:
  0.6 34.9 %shard_map.94 = (bf16[512,512]{1,0:T(8,128)(2,1)S(1)}, bf16[512,512]{1,0:T(8,128)(2,1)S(1)}, f32[4,512]{1,0:T(4,128)S(1)}) custom-call(bf16[512,512]{1,0:T(8,128)(2,1)} %q_ref.1, bf16[512,128]{1,0:T(8,128)(2,1)} %k_ref.1, bf16[512,128]{1,0:T(8,128)(2,1)} %v_ref.1, bf16[512,512]{1,0:T(8,128)(2,1)} %g_ref.1, bf16[4096,768]{1,0:T(8,128)(2,1)} %w_ref.1, ...), custom_call_target="tpu_custom_call" | custom-call | tf_op jit(solution)/shard_map/pallas_call | solution.py:384
  35.5 1.0 %shard_map.95 = (bf16[512,512]{1,0:T(8,128)(2,1)}, bf16[512,512]{1,0:T(8,128)(2,1)}, f32[4,512]{1,0:T(4,128)}) custom-call(bf16[512,512]{1,0:T(8,128)(2,1)S(1)} %get-tuple-element.6.o_ref, bf16[512,512]{1,0:T(8,128)(2,1)S(1)} %get-tuple-element.7.gi_ref, f32[4,512]{1,0:T(4,128)S(1)} %get-tuple-element.8.lse_ref), custom_call_target="tpu_custom_call" | custom-call | tf_op jit(solution)/shard_map/pallas_call | solution.py:429

commit v4 on v3

--- a/solution.py
+++ b/solution.py
@@ -36,7 +36,7 @@
 def kernel(
     q_ref, k_ref, v_ref, g_ref, w_ref, len_hbm, plan_hbm,
     o_ref, gi_ref, lse_ref,
-    kbuf, vbuf, qbuf, gbuf, wown, wpar, dkv, ret, st,
+    kbuf, vbuf, qbuf, gbuf, wown, wpar, dkv, leave, ret, st,
     s2, sp, sm, hp, hm, rp, rm, own, mp, mm,
     obuf, gibuf, lbuf, lout, len_ref, plan_ref,
     lsem, wsem, osem,
@@ -96,7 +96,7 @@
         lbuf[1] = jnp.zeros((GROUP, 512), F32)
 
     def no_return():
-        ret[...] = jnp.zeros((2, 256, 128), F32)
+        ret[...] = jnp.zeros((2, 2, 128, 128), BF16)
         lbuf[2] = jnp.zeros((GROUP, 512), F32)
 
     pl.when(jnp.logical_not(has_prev))(no_halo)
@@ -119,6 +119,8 @@
         0, len_ref.shape[0], scan_lengths, (start, start, edge, start, start, start)
     )[1:]
 
+    locals_[0].wait()
+    locals_[2].wait()
     pl.semaphore_wait(
         barrier, 3 + jnp.where(has_next, 1, 0) + jnp.where(has_prev, 1, 0)
     )
@@ -126,10 +128,10 @@
     halo = {}
     slot = 0
     for b in (1, 0):
-        for src, dst in ((k_ref, kbuf), (v_ref, vbuf)):
+        for buf in (kbuf, vbuf):
             copy = remote(
-                src.at[pl.ds(256 + b * BLOCK, BLOCK)],
-                dst.at[pl.ds(b * BLOCK, BLOCK)],
+                buf.at[pl.ds(512 + b * BLOCK, BLOCK)],
+                buf.at[pl.ds(b * BLOCK, BLOCK)],
                 halo_s.at[slot], halo_r.at[slot], nxt,
             )
             pl.when(has_next)(copy.start)
@@ -142,8 +144,8 @@
     for r in (2, 1, 3, 0):
         w_swap[r].start()
 
-    for copy in locals_:
-        copy.wait()
+    locals_[1].wait()
+    locals_[3].wait()
 
     scale = HEAD_DIM ** -0.5
     causal = lax.broadcasted_iota(jnp.int32, (BLOCK, BLOCK), 0) <= lax.broadcasted_iota(
@@ -201,7 +203,7 @@
         query_grad = (dot(keys, score_grad, ((0,), (0,))) * scale).astype(BF16)
         for h in range(GROUP):
             columns = slice(h * BLOCK, (h + 1) * BLOCK)
-            obuf[rows, pl.ds(h * HEAD_DIM, HEAD_DIM)] = out[:, columns].T
+            o_ref[rows, pl.ds(h * HEAD_DIM, HEAD_DIM)] = out[:, columns].T
             st[0, qb, :, pl.ds(h * HEAD_DIM, HEAD_DIM)] = query_grad[:, columns].T
         key_add = dot(score_grad, queries, ((1,), (0,)))
         value_add = dot(weights_low, grads, ((1,), (0,)))
@@ -214,14 +216,19 @@
         remote(st.at[0, t], st.at[1, t], st_s.at[t], st_r.at[t], par) for t in range(BLOCKS)
     ]
 
+    back_copies = [
+        remote(leave.at[b], ret.at[b], ret_s.at[b], ret_r.at[b], prv)
+        for b in range(REACH_BLOCKS)
+    ]
+
     def finish_tokens(t):
         rows = pl.ds((t + REACH_BLOCKS) * BLOCK, BLOCK)
         key_grad = dkv[0, rows, :]
         value_grad = dkv[1, rows, :]
         if t >= 2:
-            back = pl.ds((t - 2) * BLOCK, BLOCK)
-            key_grad = key_grad + ret[0, back, :]
-            value_grad = value_grad + ret[1, back, :]
+            pl.when(has_next)(back_copies[t - 2].wait_recv)
+            key_grad = key_grad + ret[t - 2, 0].astype(F32)
+            value_grad = value_grad + ret[t - 2, 1].astype(F32)
         st[0, t, :, pl.ds(GROUP * HEAD_DIM, HEAD_DIM)] = (key_grad * scale).astype(BF16)
         st[0, t, :, pl.ds((GROUP + 1) * HEAD_DIM, HEAD_DIM)] = value_grad.astype(BF16)
         st_swap[t].start()
@@ -237,14 +244,14 @@
     attend(0)
     finish_tokens(0)
 
-    back_copy = remote(dkv.at[:, pl.ds(0, 256), :], ret, ret_s, ret_r, prv)
-    pl.when(has_prev)(back_copy.start)
+    for b in range(REACH_BLOCKS):
+        for which in range(2):
+            leave[b, which] = dkv[which, pl.ds(b * BLOCK, BLOCK), :].astype(BF16)
+        pl.when(has_prev)(back_copies[b].start)
     lse_next = remote(lbuf.at[0], lbuf.at[1], lse_s.at[0], lse_r.at[0], nxt)
     lse_prev = remote(lbuf.at[0], lbuf.at[2], lse_s.at[1], lse_r.at[1], prv)
     pl.when(has_next)(lse_next.start)
     pl.when(has_prev)(lse_prev.start)
-    out_copy = pltpu.make_async_copy(obuf, o_ref, osem.at[0])
-    out_copy.start()
 
     HALF = BLOCK // 2
     lo, hi = pl.ds(0, HALF), pl.ds(HALF, HALF)
@@ -291,25 +298,19 @@
         sm[t, hi, :] = (mm[t] + hm[t].astype(F32)).astype(BF16)
         sends[t]["m_dn"].start()
 
-    gi_copies = []
-
     def finish(t):
         for name in ("u_up", "u_dn", "m_up", "m_dn"):
             sends[t][name].wait_recv()
         rows = pl.ds(t * BLOCK, BLOCK)
-        gibuf[rows, :] = (own[t] + rp[t].astype(F32) + rm[t].astype(F32)).astype(BF16)
-        copy = pltpu.make_async_copy(gibuf.at[rows], gi_ref.at[rows], osem.at[1 + t])
-        copy.start()
-        gi_copies.append(copy)
+        gi_ref[rows, :] = (own[t] + rp[t].astype(F32) + rm[t].astype(F32)).astype(BF16)
 
     project(1, True)
     project(0, False)
-    pl.when(has_next)(back_copy.wait_recv)
+    merge(1)
     finish_tokens(2)
     finish_tokens(3)
-    merge(1)
+    merge(0)
     project(2, False)
-    merge(0)
     project(3, False)
     merge(2)
 
@@ -330,18 +331,14 @@
                 picked[s] = picked[s] + piece * take
             rank = rank + hit
     for s in range(BLOCKS):
-        lout[:, pl.ds(s * BLOCK, BLOCK)] = picked[s]
-    lse_copy = pltpu.make_async_copy(lout, lse_ref, osem.at[5])
-    lse_copy.start()
-
+        lse_ref[:, pl.ds(s * BLOCK, BLOCK)] = picked[s]
+
+    finish(1)
+    finish(0)
     merge(3)
-    for t in (1, 0, 2, 3):
-        finish(t)
-
-    out_copy.wait()
-    lse_copy.wait()
-    for copy in gi_copies:
-        copy.wait()
+    finish(2)
+    finish(3)
+
     for b in (1, 0):
         for copy in halo[b]:
             pl.when(has_next)(copy.wait_send)
@@ -349,7 +346,8 @@
         copy.wait_send()
     for copy in st_swap:
         copy.wait_send()
-    pl.when(has_prev)(back_copy.wait_send)
+    for copy in back_copies:
+        pl.when(has_prev)(copy.wait_send)
     pl.when(has_next)(lse_next.wait_send)
     pl.when(has_prev)(lse_prev.wait_send)
     for t in range(BLOCKS):
@@ -385,7 +383,7 @@
         kernel,
         out_shape=shapes,
         in_specs=[anywhere] * 7,
-        out_specs=(anywhere,) * 3,
+        out_specs=(pl.BlockSpec(memory_space=pltpu.VMEM),) * 3,
         scratch_shapes=[
             pltpu.VMEM((768, 128), BF16),
             pltpu.VMEM((768, 128), BF16),
@@ -394,7 +392,8 @@
             pltpu.VMEM((4, 512, 768), BF16),
             pltpu.VMEM((4, 512, 768), BF16),
             pltpu.VMEM((2, 768, 128), F32),
-            pltpu.VMEM((2, 256, 128), F32),
+            pltpu.VMEM((2, 2, 128, 128), BF16),
+            pltpu.VMEM((2, 2, 128, 128), BF16),
             pltpu.VMEM((2, 4, 128, 768), BF16),
             pltpu.VMEM((4, 128, 512), BF16),
             pltpu.VMEM((4, 128, 512), BF16),
@@ -418,7 +417,7 @@
             dma((4,)), dma((4,)),
             dma((4,)), dma((4,)),
             dma((4,)), dma((4,)),
-            dma, dma,
+            dma((2,)), dma((2,)),
             dma((2,)), dma((2,)),
             dma((4, 6)), dma((4, 6)),
         ],

time: 36.6 us -> 34.8 us (0.951)
  the two profiles are of different devices: /device:TPU:103 before, /device:TPU:128 now
where the time goes in v4:
time: 34.8 us; the launch traced here: 34.6 us
  Pallas kernels  33.9 us (97%)
  between operations  0.64 us (2%)
    pallas_call x1, Pallas kernels, body(): pl.pallas_call(kernel, out_shape=shapes, in_specs=[anywhere] * 7, out_spe...  32.9 us
    pallas_call x1, Pallas kernels, body(): pl.pallas_call(publish, out_shape=shapes, in_specs=[anywhere] * 3, out_sp...  1.04 us

profile of v4, /device:TPU:128, one launch (start us, length us, event | category | flops | bytes accessed | tf_op | source)
XLA Modules:
  0.0 34.6 jit_solution(9894711324885900686)
XLA Ops:
  0.6 32.9 %shard_map.94 = (bf16[512,512]{1,0:T(8,128)(2,1)S(1)}, bf16[512,512]{1,0:T(8,128)(2,1)S(1)}, f32[4,512]{1,0:T(4,128)S(1)}) custom-call(bf16[512,512]{1,0:T(8,128)(2,1)} %q_ref.1, bf16[512,128]{1,0:T(8,128)(2,1)} %k_ref.1, bf16[512,128]{1,0:T(8,128)(2,1)} %v_ref.1, bf16[512,512]{1,0:T(8,128)(2,1)} %g_ref.1, bf16[4096,768]{1,0:T(8,128)(2,1)} %w_ref.1, ...), custom_call_target="tpu_custom_call" | custom-call | tf_op jit(solution)/shard_map/pallas_call | solution.py:382
  33.5 1.0 %shard_map.95 = (bf16[512,512]{1,0:T(8,128)(2,1)}, bf16[512,512]{1,0:T(8,128)(2,1)}, f32[4,512]{1,0:T(4,128)}) custom-call(bf16[512,512]{1,0:T(8,128)(2,1)S(1)} %get-tuple-element.6.o_ref, bf16[512,512]{1,0:T(8,128)(2,1)S(1)} %get-tuple-element.7.gi_ref, f32[4,512]{1,0:T(4,128)S(1)} %get-tuple-element.8.lse_ref), custom_call_target="tpu_custom_call" | custom-call | tf_op jit(solution)/shard_map/pallas_call | solution.py:428

commit v5 on v4

--- a/solution.py
+++ b/solution.py
@@ -62,15 +62,10 @@
         pl.semaphore_signal(barrier, inc=1, device_id=device, device_id_type=MESH)
 
     barrier = pltpu.get_barrier_semaphore()
+    pl.when(has_prev)(lambda: greet(prv))
     pl.when(has_next)(lambda: greet(nxt))
-    pl.when(has_prev)(lambda: greet(prv))
     for device in (par, up, dn):
         greet(device)
-    len_copy = pltpu.make_async_copy(len_hbm, len_ref, lsem.at[4])
-    plan_copy = pltpu.make_async_copy(plan_hbm, plan_ref, lsem.at[5])
-    len_copy.start()
-    plan_copy.start()
-
     locals_ = [
         pltpu.make_async_copy(k_ref, kbuf.at[pl.ds(256, 512)], lsem.at[0]),
         pltpu.make_async_copy(q_ref, qbuf, lsem.at[1]),
@@ -80,15 +75,10 @@
     for copy in locals_:
         copy.start()
 
-    def w_rows(r, c):
-        return pl.ds(pl.multiple_of((2 * lax.rem(y + r, n_y) + c) * 512, 512), 512)
-
-    w_local = [
-        pltpu.make_async_copy(w_ref.at[w_rows(r, core)], wown.at[r], wsem.at[r])
-        for r in range(4)
-    ]
-    for r in (2, 1, 3, 0):
-        w_local[r].start()
+    len_copy = pltpu.make_async_copy(len_hbm, len_ref, lsem.at[4])
+    plan_copy = pltpu.make_async_copy(plan_hbm, plan_ref, lsem.at[5])
+    len_copy.start()
+    plan_copy.start()
 
     def no_halo():
         kbuf[pl.ds(0, 256), :] = jnp.zeros((256, 128), BF16)
@@ -101,23 +91,6 @@
 
     pl.when(jnp.logical_not(has_prev))(no_halo)
     pl.when(jnp.logical_not(has_next))(no_return)
-
-    first = ctx * BLOCKS
-
-    def scan_lengths(i, carry):
-        total = carry[0] + len_ref[i]
-        return (total,) + tuple(
-            carry[1 + b] + jnp.where(total == (first + b - 1) * BLOCK, 1, 0)
-            for b in range(5)
-        )
-
-    start = jnp.int32(0)
-    edge = jnp.where(ctx == 0, 1, 0).astype(jnp.int32)
-    len_copy.wait()
-    plan_copy.wait()
-    found = lax.fori_loop(
-        0, len_ref.shape[0], scan_lengths, (start, start, edge, start, start, start)
-    )[1:]
 
     locals_[0].wait()
     locals_[2].wait()
@@ -137,12 +110,41 @@
             pl.when(has_next)(copy.start)
             halo.setdefault(b, []).append(copy)
             slot += 1
+    def w_rows(r, c):
+        return pl.ds(pl.multiple_of((2 * lax.rem(y + r, n_y) + c) * 512, 512), 512)
+
+    w_local = [
+        pltpu.make_async_copy(w_ref.at[w_rows(r, core)], wown.at[r], wsem.at[r])
+        for r in range(4)
+    ]
+    for r in (2, 1, 3, 0):
+        w_local[r].start()
     w_swap = [
         remote(w_ref.at[w_rows(r, 1 - core)], wpar.at[r], w_s.at[r], w_r.at[r], par)
         for r in range(4)
     ]
     for r in (2, 1, 3, 0):
         w_swap[r].start()
+
+    origin = (ctx * BLOCKS - 1) * BLOCK
+    len_copy.wait()
+
+    def scan_lengths(i, carry):
+        total, bits = carry
+        total = total + len_ref[i]
+        away = total - origin
+        inside = (away >= 0) & (away <= BLOCKS * BLOCK)
+        bit = jnp.left_shift(jnp.int32(1), jnp.where(inside, away // BLOCK, 0))
+        return total, bits | jnp.where(inside, bit, 0)
+
+    _, bits = lax.fori_loop(
+        0,
+        len_ref.shape[0],
+        scan_lengths,
+        (jnp.int32(0), jnp.where(ctx == 0, 2, 0).astype(jnp.int32)),
+        unroll=8,
+    )
+    found = [jnp.bitwise_and(bits, 1 << b) for b in range(BLOCKS + 1)]
 
     locals_[1].wait()
     locals_[3].wait()
@@ -169,28 +171,48 @@
             [ref[rows, pl.ds(h * HEAD_DIM, HEAD_DIM)] for h in range(GROUP)], axis=0
         )
 
-    def attend(qb):
-        rows = pl.ds(qb * BLOCK, BLOCK)
-        keys = kbuf[pl.ds(qb * BLOCK, 3 * BLOCK), :]
-        vals = vbuf[pl.ds(qb * BLOCK, 3 * BLOCK), :]
-        queries = heads_in_rows(qbuf, qb)
-        grads = heads_in_rows(gbuf, qb)
-        near = jnp.where(found[qb + 1] > 0, NEG, 0.0).astype(F32)
-        far = jnp.where(found[qb + 1] + found[qb] > 0, NEG, 0.0).astype(F32)
+    def bias_of(qb, block):
+        if block == 2:
+            return causal_bias
+        edges = found[qb + 1] if block == 1 else found[qb + 1] + found[qb]
+        return jnp.where(edges > 0, NEG, 0.0).astype(F32)
+
+    exponent = scale * LOG2E
+
+    def partial(qb, blocks, queries, grads):
+        keys = kbuf[pl.ds((qb + blocks[0]) * BLOCK, len(blocks) * BLOCK), :]
+        vals = vbuf[pl.ds((qb + blocks[0]) * BLOCK, len(blocks) * BLOCK), :]
         scores = dot(keys, queries, ((1,), (1,)))
         prob = dot(vals, grads, ((1,), (1,)))
         scores = jnp.concatenate(
             [
-                scores[:BLOCK] + far,
-                scores[BLOCK : 2 * BLOCK] + near,
-                scores[2 * BLOCK :] + causal_bias,
+                scores[i * BLOCK : (i + 1) * BLOCK] + bias_of(qb, block)
+                for i, block in enumerate(blocks)
             ],
             axis=0,
         )
-        top = jnp.max(scores, axis=0, keepdims=True)
-        raised = jnp.exp2((scores - top) * (scale * LOG2E))
+        return scores, prob, jnp.max(scores, axis=0, keepdims=True)
+
+    def begin(qb, blocks):
+        queries, grads = heads_in_rows(qbuf, qb), heads_in_rows(gbuf, qb)
+        scores, prob, top = partial(qb, blocks, queries, grads)
+        raised = jnp.exp2((scores - top) * exponent)
         total = jnp.sum(raised, axis=0, keepdims=True)
         mixed = jnp.sum(raised * prob, axis=0, keepdims=True)
+        return raised, prob, top, total, mixed
+
+    def weigh(qb, first, known=None):
+        scores, prob, top = first
+        rows = pl.ds(qb * BLOCK, BLOCK)
+        if known is not None:
+            top = jnp.maximum(top, known[2])
+        raised = jnp.exp2((scores - top) * exponent)
+        total = jnp.sum(raised, axis=0, keepdims=True)
+        mixed = jnp.sum(raised * prob, axis=0, keepdims=True)
+        if known is not None:
+            lower = jnp.exp2((known[2] - top) * exponent)
+            total = total + known[3] * lower
+            mixed = mixed + known[4] * lower
         inverse = 1.0 / total
         row_dot = mixed * inverse
         lse = top * scale + jnp.log(total)
@@ -199,18 +221,37 @@
         weights = raised * inverse
         weights_low = weights.astype(BF16)
         score_grad = (weights * (prob - row_dot)).astype(BF16)
-        out = dot(vals, weights_low, ((0,), (0,))).astype(BF16)
-        query_grad = (dot(keys, score_grad, ((0,), (0,))) * scale).astype(BF16)
-        for h in range(GROUP):
-            columns = slice(h * BLOCK, (h + 1) * BLOCK)
-            o_ref[rows, pl.ds(h * HEAD_DIM, HEAD_DIM)] = out[:, columns].T
-            st[0, qb, :, pl.ds(h * HEAD_DIM, HEAD_DIM)] = query_grad[:, columns].T
+        if known is not None:
+            weights = known[0] * (lower * inverse)
+            weights_low = jnp.concatenate([weights_low, weights.astype(BF16)], axis=0)
+            score_grad = jnp.concatenate(
+                [score_grad, (weights * (known[1] - row_dot)).astype(BF16)], axis=0
+            )
+        return weights_low, score_grad
+
+    def spread(qb, weights_low, score_grad):
+        rows = pl.ds(qb * BLOCK, BLOCK)
+        queries, grads = heads_in_rows(qbuf, qb), heads_in_rows(gbuf, qb)
+        keys = kbuf[pl.ds(qb * BLOCK, 3 * BLOCK), :]
+        vals = vbuf[pl.ds(qb * BLOCK, 3 * BLOCK), :]
         key_add = dot(score_grad, queries, ((1,), (0,)))
         value_add = dot(weights_low, grads, ((1,), (0,)))
         for b in range(3):
             part = slice(b * BLOCK, (b + 1) * BLOCK)
             add_grad(0, qb + b, key_add[part])
             add_grad(1, qb + b, value_add[part])
+        query_grad = (dot(keys, score_grad, ((0,), (0,))) * scale).astype(BF16)
+        out = dot(vals, weights_low, ((0,), (0,))).astype(BF16)
+        for h in range(GROUP):
+            columns = slice(h * BLOCK, (h + 1) * BLOCK)
+            st[0, qb, :, pl.ds(h * HEAD_DIM, HEAD_DIM)] = query_grad[:, columns].T
+            o_ref[rows, pl.ds(h * HEAD_DIM, HEAD_DIM)] = out[:, columns].T
+
+    def look(qb, blocks):
+        return partial(qb, blocks, heads_in_rows(qbuf, qb), heads_in_rows(gbuf, qb))
+
+    def attend(qb, blocks, known=None):
+        spread(qb, *weigh(qb, look(qb, blocks), known))
 
     st_swap = [
         remote(st.at[0, t], st.at[1, t], st_s.at[t], st_r.at[t], par) for t in range(BLOCKS)
@@ -233,15 +274,22 @@
         st[0, t, :, pl.ds((GROUP + 1) * HEAD_DIM, HEAD_DIM)] = value_grad.astype(BF16)
         st_swap[t].start()
 
-    attend(2)
-    attend(3)
+    look2, look3 = look(2, (0, 1, 2)), look(3, (0, 1, 2))
+    weigh2 = weigh(2, look2)
+    weigh3 = weigh(3, look3)
+    spread(2, *weigh2)
+    spread(3, *weigh3)
+    known1 = begin(1, (1, 2))
+    known0 = begin(0, (2,))
     for copy in halo[1]:
         pl.when(has_prev)(copy.wait_recv)
-    attend(1)
+    attend(1, (0,), known1)
     finish_tokens(1)
+    w_local[2].wait()
+    ahead = dot(st[0, 1], wown[2], ((1,), (1,)))
     for copy in halo[0]:
         pl.when(has_prev)(copy.wait_recv)
-    attend(0)
+    attend(0, (0, 1), known0)
     finish_tokens(0)
 
     for b in range(REACH_BLOCKS):
@@ -255,7 +303,7 @@
 
     HALF = BLOCK // 2
     lo, hi = pl.ds(0, HALF), pl.ds(HALF, HALF)
-    for r in range(4):
+    for r in (1, 3, 0):
         w_local[r].wait()
 
     sends = {}
@@ -275,7 +323,8 @@
         def part(r):
             if first_time:
                 w_swap[r].wait_recv()
-            return dot(st[0, t], wown[r], ((1,), (1,))) + dot(st[1, t], wpar[r], ((1,), (1,)))
+            mine = ahead if first_time and r == 2 else dot(st[0, t], wown[r], ((1,), (1,)))
+            return mine + dot(st[1, t], wpar[r], ((1,), (1,)))
 
         s2[t] = part(2).astype(BF16)
         sends[t]["h_up"].start()
@@ -314,6 +363,7 @@
     project(3, False)
     merge(2)
 
+    plan_copy.wait()
     pl.when(has_prev)(lse_next.wait_recv)
     pl.when(has_next)(lse_prev.wait_recv)
     picked = [jnp.zeros((GROUP, BLOCK), F32) for _ in range(BLOCKS)]

time: 34.8 us -> 34.6 us (level)
  no operation moved by 1% of the time
where the time goes in v5:
time: 34.6 us; the launch traced here: 34.4 us
  Pallas kernels  33.7 us (97%)
  between operations  0.64 us (2%)
    pallas_call x1, Pallas kernels, body(): pl.pallas_call(kernel, out_shape=shapes, in_specs=[anywhere] * 7, out_spe...  32.7 us
    pallas_call x1, Pallas kernels, body(): pl.pallas_call(publish, out_shape=shapes, in_specs=[anywhere] * 3, out_sp...  1.04 us

profile of v5, /device:TPU:128, one launch (start us, length us, event | category | flops | bytes accessed | tf_op | source)
XLA Modules:
  0.0 34.4 jit_solution(2064245580233865458)
XLA Ops:
  0.6 32.7 %shard_map.94 = (bf16[512,512]{1,0:T(8,128)(2,1)S(1)}, bf16[512,512]{1,0:T(8,128)(2,1)S(1)}, f32[4,512]{1,0:T(4,128)S(1)}) custom-call(bf16[512,512]{1,0:T(8,128)(2,1)} %q_ref.1, bf16[512,128]{1,0:T(8,128)(2,1)} %k_ref.1, bf16[512,128]{1,0:T(8,128)(2,1)} %v_ref.1, bf16[512,512]{1,0:T(8,128)(2,1)} %g_ref.1, bf16[4096,768]{1,0:T(8,128)(2,1)} %w_ref.1, ...), custom_call_target="tpu_custom_call" | custom-call | tf_op jit(solution)/shard_map/pallas_call | solution.py:432
  33.3 1.0 %shard_map.95 = (bf16[512,512]{1,0:T(8,128)(2,1)}, bf16[512,512]{1,0:T(8,128)(2,1)}, f32[4,512]{1,0:T(4,128)}) custom-call(bf16[512,512]{1,0:T(8,128)(2,1)S(1)} %get-tuple-element.6.o_ref, bf16[512,512]{1,0:T(8,128)(2,1)S(1)} %get-tuple-element.7.gi_ref, f32[4,512]{1,0:T(4,128)S(1)} %get-tuple-element.8.lse_ref), custom_call_target="tpu_custom_call" | custom-call | tf_op jit(solution)/shard_map/pallas_call | solution.py:478

commit v6 on v5

--- a/solution.py
+++ b/solution.py
@@ -298,8 +298,6 @@
         pl.when(has_prev)(back_copies[b].start)
     lse_next = remote(lbuf.at[0], lbuf.at[1], lse_s.at[0], lse_r.at[0], nxt)
     lse_prev = remote(lbuf.at[0], lbuf.at[2], lse_s.at[1], lse_r.at[1], prv)
-    pl.when(has_next)(lse_next.start)
-    pl.when(has_prev)(lse_prev.start)
 
     HALF = BLOCK // 2
     lo, hi = pl.ds(0, HALF), pl.ds(HALF, HALF)
@@ -317,7 +315,7 @@
             m_dn=remote(sm.at[t, hi], rm.at[t, hi], rs_s.at[t, 5], rs_r.at[t, 5], dn),
         )
 
-    def project(t, first_time):
+    def project(t, first_time, hold=False):
         st_swap[t].wait_recv()
 
         def part(r):
@@ -331,13 +329,23 @@
         sends[t]["h_dn"].start()
         piece = part(1)
         sp[t, hi, :] = piece[HALF:].astype(BF16)
-        sends[t]["u_up"].start()
+        if not hold:
+            sends[t]["u_up"].start()
         mp[t] = piece[:HALF]
         piece = part(3)
         sm[t, lo, :] = piece[:HALF].astype(BF16)
+        if not hold:
+            sends[t]["u_dn"].start()
+        mm[t] = piece[HALF:]
+
+    def keep(t, first_time=False):
+        if first_time:
+            w_swap[0].wait_recv()
+        own[t] = dot(st[0, t], wown[0], ((1,), (1,))) + dot(st[1, t], wpar[0], ((1,), (1,)))
+
+    def release(t):
+        sends[t]["u_up"].start()
         sends[t]["u_dn"].start()
-        mm[t] = piece[HALF:]
-        own[t] = part(0)
 
     def merge(t):
         sends[t]["h_up"].wait_recv()
@@ -354,14 +362,23 @@
         gi_ref[rows, :] = (own[t] + rp[t].astype(F32) + rm[t].astype(F32)).astype(BF16)
 
     project(1, True)
-    project(0, False)
+    pl.when(has_next)(lse_next.start)
+    pl.when(has_prev)(lse_prev.start)
+    project(0, False, True)
     merge(1)
+    release(0)
     finish_tokens(2)
     finish_tokens(3)
+    keep(1, True)
     merge(0)
-    project(2, False)
-    project(3, False)
+    keep(0)
+    project(2, False, True)
+    project(3, False, True)
     merge(2)
+    release(2)
+    release(3)
+    keep(2)
+    keep(3)
 
     plan_copy.wait()
     pl.when(has_prev)(lse_next.wait_recv)

time: 34.6 us -> 34.5 us (level)
  no operation moved by 1% of the time
where the time goes in v6:
time: 34.5 us; the launch traced here: 34.4 us
  Pallas kernels  33.8 us (98%)
  between operations  0.64 us (2%)
    pallas_call x1, Pallas kernels, body(): pl.pallas_call(kernel, out_shape=shapes, in_specs=[anywhere] * 7, out_spe...  32.7 us
    pallas_call x1, Pallas kernels, body(): pl.pallas_call(publish, out_shape=shapes, in_specs=[anywhere] * 3, out_sp...  1.04 us

profile of v6, /device:TPU:128, one launch (start us, length us, event | category | flops | bytes accessed | tf_op | source)
XLA Modules:
  0.0 34.4 jit_solution(16671881508175402862)
XLA Ops:
  0.6 32.7 %shard_map.94 = (bf16[512,512]{1,0:T(8,128)(2,1)S(1)}, bf16[512,512]{1,0:T(8,128)(2,1)S(1)}, f32[4,512]{1,0:T(4,128)S(1)}) custom-call(bf16[512,512]{1,0:T(8,128)(2,1)} %q_ref.1, bf16[512,128]{1,0:T(8,128)(2,1)} %k_ref.1, bf16[512,128]{1,0:T(8,128)(2,1)} %v_ref.1, bf16[512,512]{1,0:T(8,128)(2,1)} %g_ref.1, bf16[4096,768]{1,0:T(8,128)(2,1)} %w_ref.1, ...), custom_call_target="tpu_custom_call" | custom-call | tf_op jit(solution)/shard_map/pallas_call | solution.py:449
  33.4 1.0 %shard_map.95 = (bf16[512,512]{1,0:T(8,128)(2,1)}, bf16[512,512]{1,0:T(8,128)(2,1)}, f32[4,512]{1,0:T(4,128)}) custom-call(bf16[512,512]{1,0:T(8,128)(2,1)S(1)} %get-tuple-element.6.o_ref, bf16[512,512]{1,0:T(8,128)(2,1)S(1)} %get-tuple-element.7.gi_ref, f32[4,512]{1,0:T(4,128)S(1)} %get-tuple-element.8.lse_ref), custom_call_target="tpu_custom_call" | custom-call | tf_op jit(solution)/shard_map/pallas_call | solution.py:495
